TPU v7x, 128 devices: a whole 4x4x4 slice. The times are simulated.
128 devices in a mesh: sib: 2 (over x_lo), row: 8 (over y, core), col: 8 (over z, x_hi).
Axes of the slice: x: 4 (x_hi: 2, x_lo: 2; x = x_hi * 2 + x_lo), y: 4, z: 4, core: 2. Of those that a mesh axis runs over, the one named last changes fastest.
Arguments:
- child_tiles: float32 [2, 64, 128, 128, 128], P('sib', ('row', 'col')), may hold values from -6 to 6
- child_rows: int32 [2, 64], P('sib'), may hold values from 0 to 127, as said below
- child_slots: int32 [2, 64, 128], P('sib', ('row', 'col')), may hold values from 0 to 4095, as said below
- tile_count: int32 [2, 64], P('sib', ('row', 'col')), may hold values from 64 to 128, as said below
- inverses: float32 [2, 512, 512], replicated, as said below
Outputs:
- factored: float32 [8, 16, 16, 8, 128, 128], P(None, ('sib', 'row'), None, 'col')
Inputs may be any that keep to these rules, and one draw needn't show every extreme that they name: `child_rows`: A child's entries are distinct; entry i leaves the same remainder as i when divided by the number of grid rows of the parent. `child_slots`: call the owner of parent tile (I, J) the grid row I mod (number of grid rows) and grid column J mod (number of grid columns). Among the live slots of one device at most 2 carry tiles with one owner; in every draw some device reaches 2 for some owner. `tile_count`: some device of each child has all 128 slots live. `inverses`: each matrix is lower triangular with positive diagonal.
All inputs are finite; a program needn't handle non-finite values.
Results may differ from a plain program's by a relative error of at most 0.00012.
Values sent between devices are 32-bit elements; how exact they have to be, the bound alone decides.
No kernel may reach another device: no remote copies, remote signals or barrier semaphores. Data moves between devices by JAX's collectives and lax.ppermute only.
A program may use at most 192 MiB of HBM per device.

v0:
```python
import jax
import jax.numpy as jnp
from jax import lax
from jax.sharding import PartitionSpec as P

NF = 16384
TILE = 128
PANEL = 512
NPANEL = 2
CHILD_TILES = 64
CAP = 2


def broadcast(value, axis, source):
    kept = jnp.where(lax.axis_index(axis) == source, value, 0).astype(value.dtype)
    return lax.psum(kept, axis)


def local(child_tiles, child_rows, child_slots, tile_count, inverses):
    grid_rows = lax.axis_size("sib") * lax.axis_size("row")
    columns = lax.axis_size("col")
    devices = grid_rows * columns
    tile_order = NF // TILE
    local_rows = tile_order // grid_rows
    local_cols = tile_order // columns
    tile_data = child_tiles[0, 0]
    slot_ids = child_slots[0, 0]
    live_count = tile_count[0, 0]
    row_list = child_rows[0]
    slot_total = slot_ids.shape[0]
    child_row = slot_ids // CHILD_TILES
    child_col = slot_ids % CHILD_TILES
    positions = jnp.arange(CHILD_TILES, dtype=jnp.int32)
    parent_row = jnp.sum(
        jnp.where(child_row[:, None] == positions[None, :], row_list[None, :], 0), axis=1
    )
    parent_col = jnp.sum(
        jnp.where(child_col[:, None] == positions[None, :], row_list[None, :], 0), axis=1
    )
    owner_index = parent_row % grid_rows * columns + parent_col % columns
    target = parent_row // grid_rows * local_cols + parent_col // columns
    slot_order = jnp.arange(slot_total, dtype=jnp.int32)
    is_live = slot_order < live_count
    earlier = (
        (owner_index[:, None] == owner_index[None, :])
        & is_live[None, :]
        & (slot_order[None, :] < slot_order[:, None])
    )
    slot_rank = jnp.sum(earlier.astype(jnp.int32), axis=1)
    slot_place = jnp.where(is_live, owner_index * CAP + slot_rank, devices * CAP)
    outgoing = (
        jnp.zeros((devices * CAP, TILE, TILE), jnp.float32)
        .at[slot_place]
        .set(tile_data, mode="drop")
    )
    destined = jnp.zeros((devices * CAP,), jnp.int32).at[slot_place].set(target, mode="drop")
    arrived, landing = (
        lax.all_to_all(
            outgoing.reshape(devices, CAP, TILE, TILE),
            ("sib", "row", "col"),
            split_axis=0,
            concat_axis=0,
            tiled=True,
        ),
        lax.all_to_all(
            destined.reshape(devices, CAP),
            ("sib", "row", "col"),
            split_axis=0,
            concat_axis=0,
            tiled=True,
        ),
    )
    front_tiles = jnp.zeros((local_rows * local_cols, TILE, TILE), jnp.float32)
    front_tiles = front_tiles.at[landing.reshape(-1)].add(arrived.reshape(-1, TILE, TILE))
    front_tiles = front_tiles.reshape(local_rows, local_cols, TILE, TILE)
    my_row = lax.axis_index(("sib", "row"))
    my_col = lax.axis_index("col")
    panel_tiles = PANEL // TILE
    root_count = grid_rows // columns
    tile_ids = jnp.arange(local_rows, dtype=jnp.int32) * grid_rows + my_row
    for panel_step in range(NPANEL):
        first_tile = panel_tiles * panel_step
        below_tile = first_tile + panel_tiles
        column_slot = first_tile // columns
        start_col = first_tile % columns
        is_below = tile_ids >= below_tile
        weights = inverses[panel_step]
        column_block = front_tiles[:, column_slot]
        holds_panel = (my_col >= start_col) & (my_col < start_col + panel_tiles)
        offset = jnp.clip(my_col - start_col, 0, panel_tiles - 1)
        everyone = lax.all_gather(column_block[None], "col", axis=0, tiled=True)
        chosen = everyone[start_col : start_col + panel_tiles]
        panel_rows = chosen.transpose(1, 2, 0, 3).reshape(local_rows * TILE, PANEL)
        factor = jnp.dot(panel_rows, weights.T, precision=lax.Precision.HIGHEST)
        factor = (
            factor.reshape(local_rows, TILE, PANEL) * is_below.astype(jnp.float32)[:, None, None]
        )
        panel_piece = lax.dynamic_slice_in_dim(factor, offset * TILE, TILE, 2)
        replace = is_below[:, None, None] & holds_panel
        front_tiles = front_tiles.at[:, column_slot].set(
            jnp.where(replace, panel_piece, column_block)
        )
        received = [
            broadcast(factor, ("sib", "row"), root_step * columns + my_col)
            for root_step in range(root_count)
        ]
        column_factor = jnp.stack(received, 1).reshape(local_cols, TILE, PANEL)
        front_tiles = front_tiles - jnp.einsum(
            "aip,bjp->abij", factor, column_factor, precision=lax.Precision.HIGHEST
        )
    return front_tiles.reshape(local_rows, 1, local_cols, 1, TILE, TILE)


def solution(mesh):
    return jax.shard_map(
        local,
        mesh=mesh,
        in_specs=(
            P("sib", ("row", "col"), None, None, None),
            P("sib", None),
            P("sib", ("row", "col"), None),
            P("sib", ("row", "col")),
            P(),
        ),
        out_specs=P(None, ("sib", "row"), None, "col", None, None),
        check_vma=False,
    )
```

profile of v0, /device:TPU:0, one launch (start us, length us, event | category | flops | bytes accessed | tf_op | source)
XLA Modules:
  0.0 837.8 jit_solution(17602744139437200190)
XLA Ops:
  10.6 11.1 %all-to-all-start = ((s32[128,1,2]{2,1,0:T(1,128)}), s32[128,1,2]{2,1,0:T(1,128)S(1)}, u32[]{:S(2)}, u32[]{:S(2)}) async-start(s32[128,1,2]{2,1,0:T(1,128)} %bitcast.7), calls=%async_computation | async-start | bytes 131072 | tf_op jit(solution)/shard_map/all_to_all | solution.py:65
  21.7 7.9 broadcast_in_dim.69
  29.6 23.2 %scatter_fusion = f32[256,128,128]{2,1,0:T(8,128)} fusion(f32[256,128,128]{2,1,0:T(8,128)} %broadcast_in_dim.69, s32[128]{0:T(128)S(1)} %fusion.16, f32[128,128,128]{2,1,0:T(8,128)} %bitcast.120), kind=kCustom, calls=%fused_computation.1 | custom fusion | bytes 25166336 | tf_op jit(solution)/shard_map/scatter | solution.py:54
  52.8 10.2 %all-to-all-start.1 = ((f32[128,2,128,128]{3,2,1,0:T(8,128)}), f32[128,2,128,128]{3,2,1,0:T(8,128)}, u32[]{:S(2)}, u32[]{:S(2)}) async-start(f32[128,2,128,128]{3,2,1,0:T(8,128)} %bitcast.117), calls=%async_computation.1 | async-start | bytes 33554432 | tf_op jit(solution)/shard_map/all_to_all | solution.py:58
  64.6 222.0 %all-to-all-done.1 = f32[128,2,128,128]{3,2,1,0:T(8,128)} async-done(((f32[128,2,128,128]{3,2,1,0:T(8,128)}), f32[128,2,128,128]{3,2,1,0:T(8,128)}, u32[]{:S(2)}, u32[]{:S(2)}) %all-to-all-start.1) | async-done | bytes 16777248 | tf_op jit(solution)/shard_map/all_to_all | solution.py:58
  286.6 4.5 broadcast_in_dim.64
  291.0 51.2 %scatter_fusion.1 = f32[128,128,128]{2,1,0:T(8,128)} fusion(f32[128,128,128]{2,1,0:T(8,128)} %broadcast_in_dim.64, s32[256]{0:T(256)S(1)} %bitcast.125, f32[256,128,128]{2,1,0:T(8,128)} %bitcast.11), kind=kCustom, calls=%fused_computation.2 | custom fusion | flops 4194304 | bytes 50332672 | tf_op jit(solution)/shard_map/scatter-add | solution.py:74
  342.2 1.9 slice_bitcast_fusion.1
  344.3 85.3 %all-gather.5.cloned.1.call-done = f32[64,1,128,128]{3,2,1,0:T(8,128)} async-done(((f32[8,1,128,128]{3,2,1,0:T(8,128)}), f32[64,1,128,128]{3,2,1,0:T(8,128)}) %all-gather.5.cloned.1.call-update) | async-done | bytes 4194320 | tf_op jit(solution)/shard_map/all_gather | solution.py:91
  434.4 5.3 convolution_multiply_fusion.1
  439.7 2.6 select_bitcast_fusion.3
  442.8 7.7 copy.36
  451.4 118.5 %all-reduce.7.cloned.1.call-done = (f32[8,1,128,512]{3,2,0,1:T(8,128)}, f32[8,1,128,512]{3,2,0,1:T(8,128)}) async-done(((f32[8,1,128,512]{3,2,0,1:T(8,128)}, f32[8,1,128,512]{3,2,0,1:T(8,128)}), (f32[8,1,128,512]{3,2,0,1:T(8,128)}, f32[8,1,128,512]{3,2,0,1:T(8,128)})) %all-reduce.7.cloned.1.call-update) | async-done | bytes 4194320 | tf_op jit(solution)/shard_map/psum | solution.py:16
  570.0 2.9 pad_maximum_fusion
  573.5 15.8 %bitcast_subtract_fusion.1 = f32[8,16,128,128]{3,2,0,1:T(8,128)S(1)} fusion(f32[8,16,128,128]{3,2,0,1:T(8,128)} %bitcast_dynamic-update-slice_fusion.1, f32[16,128,512,1]{2,1,3,0:T(8,128)S(1)} %bitcast.118, f32[8,128,512]{2,1,0:T(8,128)S(1)} %convolution_multiply_fusion.1), kind=kOutput, calls=%fused_computation.5 | convolution fusion | flops 12886999040 | bytes 23068672 | tf_op jit(solution)/shard_map/aip,bjp->abij/dot_general | solution.py:108
  589.4 3.4 copy-done
  593.8 72.4 %all-gather.7.cloned.1.call-done = f32[64,1,128,128]{3,2,1,0:T(8,128)} async-done(((f32[8,1,128,128]{3,2,1,0:T(8,128)}), f32[64,1,128,128]{3,2,1,0:T(8,128)}) %all-gather.7.cloned.1.call-update) | async-done | bytes 4194320 | tf_op jit(solution)/shard_map/all_gather | solution.py:91
  669.1 2.0 dot_general.19
  671.1 5.3 convolution_multiply_fusion
  676.4 2.6 select_bitcast_fusion.1
  680.0 126.6 %all-reduce.5.cloned.1.call-done = (f32[8,1,128,512]{3,2,0,1:T(8,128)}, f32[8,1,128,512]{3,2,0,1:T(8,128)}) async-done(((f32[8,1,128,512]{3,2,0,1:T(8,128)}, f32[8,1,128,512]{3,2,0,1:T(8,128)}), (f32[8,1,128,512]{3,2,0,1:T(8,128)}, f32[8,1,128,512]{3,2,0,1:T(8,128)})) %all-reduce.5.cloned.1.call-update) | async-done | bytes 4194320 | tf_op jit(solution)/shard_map/psum | solution.py:16
  806.6 3.1 pad_maximum_fusion.1
  812.0 15.0 %fusion = f32[8,1,16,1,128,128]{5,4,0,2,3,1:T(8,128)S(1)} fusion(f32[8,16,128,128]{3,2,0,1:T(8,128)S(1)} %bitcast.116, f32[16,128,512,1]{2,1,3,0:T(8,128)S(1)} %bitcast.119, f32[8,128,512]{2,1,0:T(8,128)S(1)} %convolution_multiply_fusion), kind=kOutput, calls=%fused_computation.4 | convolution fusion | flops 12886999040 | bytes 23068672 | tf_op jit(solution)/shard_map/aip,bjp->abij/dot_general | solution.py:108
  827.0 4.0 copy.43
  (41 shorter events, 18.9 us)
Async XLA Ops:
  10.6 42.2 %all-to-all-start = ((s32[128,1,2]{2,1,0:T(1,128)}), s32[128,1,2]{2,1,0:T(1,128)S(1)}, u32[]{:S(2)}, u32[]{:S(2)}) async-start(s32[128,1,2]{2,1,0:T(1,128)} %bitcast.7), calls=%async_computation | async-start | bytes 131072 | tf_op jit(solution)/shard_map/all_to_all | solution.py:65
  52.8 233.7 %all-to-all-start.1 = ((f32[128,2,128,128]{3,2,1,0:T(8,128)}), f32[128,2,128,128]{3,2,1,0:T(8,128)}, u32[]{:S(2)}, u32[]{:S(2)}) async-start(f32[128,2,128,128]{3,2,1,0:T(8,128)} %bitcast.117), calls=%async_computation.1 | async-start | bytes 33554432 | tf_op jit(solution)/shard_map/all_to_all | solution.py:58
  63.0 366.5 %all-gather.5.cloned.1.call-start = ((), (), s32[]{:S(2)}) async-start(), calls=%async_computation.2 | async-start | bytes 4718592 | tf_op jit(solution)/shard_map/all_gather | solution.py:91
  344.2 225.8 %all-reduce.7.cloned.1.call-start = ((), (), s32[]{:S(2)}) async-start(), calls=%async_computation.5 | async-start | bytes 8388608 | tf_op jit(solution)/shard_map/psum | solution.py:16
  429.5 1.6 slice-start.2
  442.3 223.9 %all-gather.7.cloned.1.call-start = ((), (), s32[]{:S(2)}) async-start(), calls=%async_computation.3 | async-start | bytes 4718592 | tf_op jit(solution)/shard_map/all_gather | solution.py:91
  589.4 3.4 copy-start
  593.7 212.9 %all-reduce.5.cloned.1.call-start = ((), (), s32[]{:S(2)}) async-start(), calls=%async_computation.4 | async-start | bytes 8388608 | tf_op jit(solution)/shard_map/psum | solution.py:16
  666.1 1.6 slice-start.3
  806.6 3.7 slice-start
  809.7 2.3 slice-start.1
Sparse Core Ops, SparseCore 0:
  344.3 85.1 all-gather.4
  442.4 127.5 all-reduce.6
  593.8 72.2 all-gather.6
  679.2 127.3 all-reduce.4
where the time goes:
time: 847 us; the launch traced here: 838 us
  waiting for transfers between devices  625 us (74%)
  local copies, waits for them, and re-layouts  68.5 us (8%)
  other arithmetic  66.7 us (8%)
  matrix products  41.5 us (5%)
  starting transfers between devices  22 us (3%)
  between operations  14.2 us (2%)
    psum x2, waiting for transfers between devices, broadcast(): return lax.psum(kept, axis)  245 us
    all_to_all x1, waiting for transfers between devices, local(): lax.all_to_all(outgoing.reshape(devices, CAP, TILE, TILE), ('sib', 'row',...  222 us
    all_gather x2, waiting for transfers between devices, local(): everyone = lax.all_gather(column_block[None], 'col', axis=0, tiled=True)  158 us
    scatter-add x1, other arithmetic, local(): front_tiles.at[landing.reshape(-1)].add(arrived.reshape(-1, TILE, TILE))  51.2 us
    dot_general x2, matrix products, local(): jnp.einsum('aip,bjp->abij', factor, column_factor, precision=lax.Precisio...  30.9 us
    scatter x1, local copies, waits for them, and re-layouts, local(): outgoing = jnp.zeros((devices * CAP, TILE, TILE), jnp.float32).at[slot_pl...  23.2 us
  transfers between devices with their start and end apart: 6, of which 5 were waited for; matrix products, arithmetic and copies ran while one was open for 5% of the time, Pallas kernels for 0%

commit v1 on v0

--- a/solution.py
+++ b/solution.py
@@ -88,7 +88,10 @@
         column_block = front_tiles[:, column_slot]
         holds_panel = (my_col >= start_col) & (my_col < start_col + panel_tiles)
         offset = jnp.clip(my_col - start_col, 0, panel_tiles - 1)
-        everyone = lax.all_gather(column_block[None], "col", axis=0, tiled=True)
+        everyone = jnp.concatenate(
+            lax.all_to_all(jnp.stack([column_block[None]] * lax.axis_size("col")), "col", 0, 0),
+            axis=0,
+        )
         chosen = everyone[start_col : start_col + panel_tiles]
         panel_rows = chosen.transpose(1, 2, 0, 3).reshape(local_rows * TILE, PANEL)
         factor = jnp.dot(panel_rows, weights.T, precision=lax.Precision.HIGHEST)

time: 847 us -> 807 us (0.953)
  waiting for transfers between devices: 625 us -> 568 us
  starting transfers between devices: 22 us -> 44.6 us
    all_gather x2 -> x0, waiting for transfers between devices: 158 us -> none  [local(): everyone = lax.all_gather(column_block[None], 'col', axis=0, tiled=True)]
    all_to_all x0 -> x2, waiting for transfers between devices: none -> 101 us  [local(): lax.all_to_all(jnp.stack([column_block[None]] * lax.axis_size('col')), 'c...]
    all_to_all x0 -> x2, starting transfers between devices: none -> 22.9 us  [local(): lax.all_to_all(jnp.stack([column_block[None]] * lax.axis_size('col')), 'c...]
    slice x8 -> x0, local copies, waits for them, and re-layouts: 8.72 us -> none  [the longest x6 5.89 us: local(): chosen = everyone[start_col:start_col + panel_tiles]]
where the time goes in v1:
time: 807 us; the launch traced here: 797 us
  waiting for transfers between devices  568 us (70%)
  other arithmetic  66.7 us (8%)
  local copies, waits for them, and re-layouts  61.9 us (8%)
  starting transfers between devices  44.6 us (6%)
  matrix products  42 us (5%)
  between operations  14.5 us (2%)
    psum x2, waiting for transfers between devices, broadcast(): return lax.psum(kept, axis)  244 us
    all_to_all x1, waiting for transfers between devices, local(): lax.all_to_all(outgoing.reshape(devices, CAP, TILE, TILE), ('sib', 'row',...  222 us
    all_to_all x2, waiting for transfers between devices, local(): lax.all_to_all(jnp.stack([column_block[None]] * lax.axis_size('col')), 'c...  101 us
    scatter-add x1, other arithmetic, local(): front_tiles.at[landing.reshape(-1)].add(arrived.reshape(-1, TILE, TILE))  51.2 us
    dot_general x2, matrix products, local(): jnp.einsum('aip,bjp->abij', factor, column_factor, precision=lax.Precisio...  31.3 us
    scatter x1, local copies, waits for them, and re-layouts, local(): outgoing = jnp.zeros((devices * CAP, TILE, TILE), jnp.float32).at[slot_pl...  23.3 us
    all_to_all x2, starting transfers between devices, local(): lax.all_to_all(jnp.stack([column_block[None]] * lax.axis_size('col')), 'c...  22.9 us
  transfers between devices with their start and end apart: 6, of which 5 were waited for; matrix products, arithmetic and copies ran while one was open for 5% of the time, Pallas kernels for 0%

profile of v1, /device:TPU:0, one launch (start us, length us, event | category | flops | bytes accessed | tf_op | source)
XLA Modules:
  0.0 797.3 jit_solution(14512053462493739376)
XLA Ops:
  10.6 11.1 %all-to-all-start = ((s32[128,1,2]{2,1,0:T(1,128)}), s32[128,1,2]{2,1,0:T(1,128)S(1)}, u32[]{:S(2)}, u32[]{:S(2)}) async-start(s32[128,1,2]{2,1,0:T(1,128)} %bitcast.7), calls=%async_computation | async-start | bytes 131072 | tf_op jit(solution)/shard_map/all_to_all | solution.py:65
  21.7 7.8 broadcast_in_dim.69
  29.6 23.3 %scatter_fusion = f32[256,128,128]{2,1,0:T(8,128)} fusion(f32[256,128,128]{2,1,0:T(8,128)} %broadcast_in_dim.69, s32[128]{0:T(128)S(1)} %fusion.28, f32[128,128,128]{2,1,0:T(8,128)} %bitcast.126), kind=kCustom, calls=%fused_computation.1 | custom fusion | bytes 25166336 | tf_op jit(solution)/shard_map/scatter | solution.py:54
  52.8 10.3 %all-to-all-start.1 = ((f32[128,2,128,128]{3,2,1,0:T(8,128)}), f32[128,2,128,128]{3,2,1,0:T(8,128)}, u32[]{:S(2)}, u32[]{:S(2)}) async-start(f32[128,2,128,128]{3,2,1,0:T(8,128)} %bitcast.123), calls=%async_computation.1 | async-start | bytes 33554432 | tf_op jit(solution)/shard_map/all_to_all | solution.py:58
  64.6 222.0 %all-to-all-done.1 = f32[128,2,128,128]{3,2,1,0:T(8,128)} async-done(((f32[128,2,128,128]{3,2,1,0:T(8,128)}), f32[128,2,128,128]{3,2,1,0:T(8,128)}, u32[]{:S(2)}, u32[]{:S(2)}) %all-to-all-start.1) | async-done | bytes 16777248 | tf_op jit(solution)/shard_map/all_to_all | solution.py:58
  286.7 4.5 broadcast_in_dim.64
  291.1 51.2 %scatter_fusion.1 = f32[128,128,128]{2,1,0:T(8,128)} fusion(f32[128,128,128]{2,1,0:T(8,128)} %broadcast_in_dim.64, s32[256]{0:T(256)S(1)} %bitcast.127, f32[256,128,128]{2,1,0:T(8,128)} %bitcast.11), kind=kCustom, calls=%fused_computation.2 | custom fusion | flops 4194304 | bytes 50332672 | tf_op jit(solution)/shard_map/scatter-add | solution.py:74
  345.8 16.3 %all-to-all-start.2 = ((f32[8,1,8,128,128]{4,3,2,1,0:T(8,128)}), f32[8,1,8,128,128]{4,3,2,1,0:T(8,128)}, u32[]{:S(2)}, u32[]{:S(2)}) async-start(f32[8,1,8,128,128]{4,3,2,1,0:T(8,128)} %stack.24), calls=%async_computation.2 | async-start | bytes 8388608 | tf_op jit(solution)/shard_map/all_to_all | solution.py:92
  362.2 51.4 %all-to-all-done.2 = f32[8,1,8,128,128]{4,3,2,1,0:T(8,128)} async-done(((f32[8,1,8,128,128]{4,3,2,1,0:T(8,128)}), f32[8,1,8,128,128]{4,3,2,1,0:T(8,128)}, u32[]{:S(2)}, u32[]{:S(2)}) %all-to-all-start.2) | async-done | bytes 4194336 | tf_op jit(solution)/shard_map/all_to_all | solution.py:92
  413.6 5.3 fusion.9
  418.9 2.6 select_bitcast_fusion.3
  421.6 7.7 copy.29
  430.2 119.7 %all-reduce.7.cloned.1.call-done = (f32[8,1,128,512]{3,2,0,1:T(8,128)}, f32[8,1,128,512]{3,2,0,1:T(8,128)}) async-done(((f32[8,1,128,512]{3,2,0,1:T(8,128)}, f32[8,1,128,512]{3,2,0,1:T(8,128)}), (f32[8,1,128,512]{3,2,0,1:T(8,128)}, f32[8,1,128,512]{3,2,0,1:T(8,128)})) %all-reduce.7.cloned.1.call-update) | async-done | bytes 4194320 | tf_op jit(solution)/shard_map/psum | solution.py:16
  549.9 2.9 pad_maximum_fusion
  553.4 16.3 %bitcast_subtract_fusion.1 = f32[8,16,128,128]{3,2,0,1:T(8,128)S(1)} fusion(f32[8,16,128,128]{3,2,0,1:T(8,128)} %bitcast_dynamic-update-slice_fusion.1, f32[16,128,512,1]{2,1,3,0:T(8,128)S(1)} %bitcast.124, f32[8,128,512]{2,1,0:T(8,128)S(1)} %fusion.9), kind=kOutput, calls=%fused_computation.5 | convolution fusion | flops 12886999040 | bytes 23068672 | tf_op jit(solution)/shard_map/aip,bjp->abij/dot_general | solution.py:111
  569.8 3.4 copy-done
  575.7 6.6 all-to-all-start.3
  582.4 50.0 %all-to-all-done.3 = f32[8,1,8,128,128]{4,3,2,1,0:T(8,128)} async-done(((f32[8,1,8,128,128]{4,3,2,1,0:T(8,128)}), f32[8,1,8,128,128]{4,3,2,1,0:T(8,128)}, u32[]{:S(2)}, u32[]{:S(2)}) %all-to-all-start.3) | async-done | bytes 4194336 | tf_op jit(solution)/shard_map/all_to_all | solution.py:92
  632.5 5.3 fusion.12
  637.8 2.6 select_bitcast_fusion.1
  641.4 124.4 %all-reduce.5.cloned.1.call-done = (f32[8,1,128,512]{3,2,0,1:T(8,128)}, f32[8,1,128,512]{3,2,0,1:T(8,128)}) async-done(((f32[8,1,128,512]{3,2,0,1:T(8,128)}, f32[8,1,128,512]{3,2,0,1:T(8,128)}), (f32[8,1,128,512]{3,2,0,1:T(8,128)}, f32[8,1,128,512]{3,2,0,1:T(8,128)})) %all-reduce.5.cloned.1.call-update) | async-done | bytes 4194320 | tf_op jit(solution)/shard_map/psum | solution.py:16
  765.8 3.1 pad_maximum_fusion.1
  771.2 15.0 %fusion = f32[8,1,16,1,128,128]{5,4,0,2,3,1:T(8,128)S(1)} fusion(f32[8,16,128,128]{3,2,0,1:T(8,128)S(1)} %bitcast.122, f32[16,128,512,1]{2,1,3,0:T(8,128)S(1)} %bitcast.125, f32[8,128,512]{2,1,0:T(8,128)S(1)} %fusion.12), kind=kOutput, calls=%fused_computation.4 | convolution fusion | flops 12886999040 | bytes 23068672 | tf_op jit(solution)/shard_map/aip,bjp->abij/dot_general | solution.py:111
  786.2 4.0 copy.35
  (34 shorter events, 15.9 us)
Async XLA Ops:
  10.6 42.3 %all-to-all-start = ((s32[128,1,2]{2,1,0:T(1,128)}), s32[128,1,2]{2,1,0:T(1,128)S(1)}, u32[]{:S(2)}, u32[]{:S(2)}) async-start(s32[128,1,2]{2,1,0:T(1,128)} %bitcast.7), calls=%async_computation | async-start | bytes 131072 | tf_op jit(solution)/shard_map/all_to_all | solution.py:65
  52.8 233.8 %all-to-all-start.1 = ((f32[128,2,128,128]{3,2,1,0:T(8,128)}), f32[128,2,128,128]{3,2,1,0:T(8,128)}, u32[]{:S(2)}, u32[]{:S(2)}) async-start(f32[128,2,128,128]{3,2,1,0:T(8,128)} %bitcast.123), calls=%async_computation.1 | async-start | bytes 33554432 | tf_op jit(solution)/shard_map/all_to_all | solution.py:58
  345.8 67.8 %all-to-all-start.2 = ((f32[8,1,8,128,128]{4,3,2,1,0:T(8,128)}), f32[8,1,8,128,128]{4,3,2,1,0:T(8,128)}, u32[]{:S(2)}, u32[]{:S(2)}) async-start(f32[8,1,8,128,128]{4,3,2,1,0:T(8,128)} %stack.24), calls=%async_computation.2 | async-start | bytes 8388608 | tf_op jit(solution)/shard_map/all_to_all | solution.py:92
  362.2 187.7 %all-reduce.7.cloned.1.call-start = ((), (), s32[]{:S(2)}) async-start(), calls=%async_computation.5 | async-start | bytes 8388608 | tf_op jit(solution)/shard_map/psum | solution.py:16
  569.7 3.4 copy-start
  575.7 56.8 %all-to-all-start.3 = ((f32[8,1,8,128,128]{4,3,2,1,0:T(8,128)}), f32[8,1,8,128,128]{4,3,2,1,0:T(8,128)}, u32[]{:S(2)}, u32[]{:S(2)}) async-start(f32[8,1,8,128,128]{4,3,2,1,0:T(8,128)} %stack.28), calls=%async_computation.3 | async-start | bytes 8388608 | tf_op jit(solution)/shard_map/all_to_all | solution.py:92
  582.2 183.6 %all-reduce.5.cloned.1.call-start = ((), (), s32[]{:S(2)}) async-start(), calls=%async_computation.4 | async-start | bytes 8388608 | tf_op jit(solution)/shard_map/psum | solution.py:16
  765.8 3.7 slice-start
  768.9 2.3 slice-start.1
Sparse Core Ops, SparseCore 0:
  421.7 128.1 all-reduce.6
  640.6 125.2 all-reduce.4
